TPU v7x, 32 devices: a whole 2x2x4 slice. The times are simulated.
32 devices in a mesh: pipe: 8 (over z, y), expert: 4 (over x, core).
Axes of the slice: x: 2, y: 2, z: 4, core: 2. Of those that a mesh axis runs over, the one named last changes fastest.
Arguments:
- saved: bfloat16 [2, 512, 6144], P(None, 'expert', 'pipe'), may hold values from -6 to 6
- top_grad: bfloat16 [2, 512, 6144], P(None, 'expert', 'pipe'), may hold values from -6 to 6
- norm_gain: float32 [6144], P('pipe'), may hold values from 0.1 to 1.9
- w_gate: bfloat16 [4, 6144, 8192], P('expert', None, 'pipe'), may hold values from -0.078125 to 0.078125
- w_up: bfloat16 [4, 6144, 8192], P('expert', None, 'pipe'), may hold values from -0.078125 to 0.078125
- w_down: bfloat16 [4, 8192, 6144], P('expert', 'pipe'), may hold values from -0.0625 to 0.0625
- routes: int32 [2, 512, 2], P(None, 'expert'), may hold values from 0 to 3, all different within a row; in each aligned block of 128 rows (0 to 127, 128 to 255, ..., all dimensions but the last counted through in order) at most 96 rows name the same one
- gates: float32 [2, 512, 2], P(None, 'expert'), may hold values from 0.1 to 0.9
Outputs:
- input_grads: float32 [2, 512, 6144], P(None, 'expert', 'pipe')
- grad_gain: float32 [6144], P('pipe')
Inputs may be any that keep to these rules, and one draw needn't show every extreme that they name: `routes`: each token names two different experts; in every aligned block of 128 rows of one micro-batch no expert is named more than 96 times, a bound that some block reaches.
All inputs are finite; a program needn't handle non-finite values.
Results may differ from a plain program's by a relative error of at most 0.017.
Values may be sent and summed in bfloat16 or wider, within the bound.
A program may use at most 128 MiB of HBM per device.

v0:
```python
import jax
import jax.numpy as jnp
from jax import lax
from jax.sharding import PartitionSpec as P

eps = 1e-05


def slot_matrix(route_block, n_experts, capacity):
    flat = route_block.reshape(-1)
    onehot = (flat[:, None] == jnp.arange(n_experts, dtype=jnp.int32)[None, :]).astype(jnp.int32)
    before = jnp.cumsum(onehot, axis=0) - onehot
    slot = jnp.sum(before * onehot, axis=1)
    target = flat * capacity + slot
    return (target[None, :] == jnp.arange(n_experts * capacity, dtype=jnp.int32)[:, None]).astype(
        jnp.bfloat16
    )


def contract_last(left, right):
    return lax.dot_general(
        left, right, (((1,), (1,)), ((), ())), preferred_element_type=jnp.float32
    )


def body(saved, top_grad, norm_gain, w_gate, w_up, w_down, routes, gates):
    n_pipe = lax.axis_size("pipe")
    n_experts = lax.axis_size("expert")
    micro, tok, part = saved.shape
    width = part * n_pipe
    capacity = 3 * tok // n_experts
    slots = n_experts * capacity
    wg = w_gate[0]
    wu = w_up[0]
    down_weight = w_down[0]
    hidden_width = wg.shape[1]
    inputs = saved.astype(jnp.float32)
    upstream = top_grad.astype(jnp.float32)
    squares = lax.psum(jnp.sum(inputs * inputs, axis=-1), "pipe")
    scale = lax.rsqrt(squares / width + eps)[:, :, None]
    normed = (inputs * scale * norm_gain).astype(jnp.bfloat16)
    placing = jax.vmap(lambda block: slot_matrix(block, n_experts, capacity))(routes)
    pair_grad = (
        (gates[:, :, :, None] * upstream[:, :, None, :])
        .reshape(micro, 2 * tok, part)
        .astype(jnp.bfloat16)
    )
    sent_x = jnp.einsum(
        "msp,mpd->msd", placing, jnp.repeat(normed, 2, axis=1), preferred_element_type=jnp.float32
    ).astype(jnp.bfloat16)
    sent_g = jnp.einsum(
        "msp,mpd->msd", placing, pair_grad, preferred_element_type=jnp.float32
    ).astype(jnp.bfloat16)
    got_x, got_g = (
        lax.all_to_all(sent_x, "expert", split_axis=1, concat_axis=1, tiled=True),
        lax.all_to_all(sent_g, "expert", split_axis=1, concat_axis=1, tiled=True),
    )
    input_slice = lax.all_gather(got_x, "pipe", axis=2, tiled=True)
    gradient_slice = lax.all_gather(got_g, "pipe", axis=2, tiled=True)
    gate_weight_rows = wg
    up_weight_rows = wu
    gate_partial_total = jnp.einsum(
        "wsk,kz->wsz", input_slice, gate_weight_rows, preferred_element_type=jnp.float32
    )
    up_partial_total = jnp.einsum(
        "wsk,kz->wsz", input_slice, up_weight_rows, preferred_element_type=jnp.float32
    )
    hidden_partial_total = jnp.einsum(
        "vun,zn->vuz", gradient_slice, down_weight, preferred_element_type=jnp.float32
    )
    sig = jax.nn.sigmoid(gate_partial_total)
    act = gate_partial_total * sig
    d_a = (
        hidden_partial_total * up_partial_total * sig * (1.0 + gate_partial_total * (1.0 - sig))
    ).astype(jnp.bfloat16)
    d_b = (hidden_partial_total * act).astype(jnp.bfloat16)
    flat_a = d_a.reshape(micro * slots, hidden_width)
    flat_b = d_b.reshape(micro * slots, hidden_width)
    gate_weight_rows = wg
    up_weight_rows = wu
    summed = lax.psum_scatter(
        (contract_last(gate_weight_rows, flat_a) + contract_last(up_weight_rows, flat_b)).astype(
            jnp.bfloat16
        ),
        "pipe",
        scatter_dimension=0,
        tiled=True,
    )
    d_rows = summed.reshape(part, micro, slots)
    returned = lax.all_to_all(d_rows, "expert", split_axis=2, concat_axis=2, tiled=True)
    d_pairs = jnp.einsum("dms,msp->mpd", returned, placing, preferred_element_type=jnp.float32)
    d_norm = d_pairs.reshape(micro, tok, 2, part).sum(axis=2)
    scaled = norm_gain * d_norm
    inner = lax.psum(jnp.sum(scaled * inputs, axis=-1), "pipe")
    d_x = scale * scaled - inputs * scale**3 * (inner / width)[:, :, None]
    input_grads = upstream + d_x
    gain_part = jnp.sum(d_norm * inputs * scale, axis=(0, 1))
    grad_gain = lax.psum(gain_part, "expert")
    return (input_grads, grad_gain)


def solution(mesh):
    placed = (
        P(None, "expert", "pipe"),
        P(None, "expert", "pipe"),
        P("pipe"),
        P("expert", None, "pipe"),
        P("expert", None, "pipe"),
        P("expert", "pipe", None),
        P(None, "expert", None),
        P(None, "expert", None),
    )
    return jax.shard_map(
        body,
        mesh=mesh,
        in_specs=placed,
        out_specs=(P(None, "expert", "pipe"), P("pipe")),
        check_vma=False,
    )
```

profile of v0, /device:TPU:0, one launch (start us, length us, event | category | flops | bytes accessed | tf_op | source)
XLA Modules:
  0.0 620.6 jit_solution(3791522047695982763)
XLA Ops:
  7.2 0.0 all-gather.5.cloned.1.call-start
  7.2 0.8 copy.21
  8.0 0.1 reshape.55
  8.2 0.1 eq.39
  8.3 1.2 fusion.17
  9.5 23.1 %psum.21 = f32[2,128]{1,0:T(2,128)S(1)} all-reduce(f32[2,128]{1,0:T(2,128)S(1)} %fusion.17), channel_id=1, replica_groups=mesh['pipe'=8,'expert'=4] {'pipe'}, use_global_device_ids=true, to_apply=%region_1.0 | all-reduce | flops 256 | bytes 2048 | tf_op jit(solution)/shard_map/psum | solution.py:39
  32.6 2.4 reduce-window.6
  35.0 0.1 slice.8
  35.1 0.1 copy.23
  35.3 0.1 copy.24
  35.4 0.1 broadcast_add_fusion
  35.5 1.2 fusion.19
  36.7 0.4 broadcast_in_dim.2
  37.1 0.3 reshape.57
  37.4 0.6 convolution_convert_fusion
  38.0 1.2 copy.30
  39.3 18.6 %all_to_all.15 = bf16[2,384,768]{2,0,1:T(2,128)(2,1)S(1)} all-to-all(bf16[2,384,768]{2,0,1:T(2,128)(2,1)S(1)} %copy.30), channel_id=1, replica_groups=mesh['pipe'=8,'expert'=4] {'expert'}, dimensions={1} | all-to-all | bytes 2359296 | tf_op jit(solution)/shard_map/all_to_all | solution.py:55
  57.8 1.2 copy.31
  59.0 0.0 all-gather.5.cloned.1.call-update
  59.0 0.0 all-gather.3.cloned.1.call-start
  59.1 0.1 copy.25
  59.2 0.1 mul.114
  59.4 0.4 mul.116
  59.8 1.1 mul.117
  60.9 0.7 convolution_convert_fusion.1
  61.5 1.2 copy.27
  62.8 18.3 %all_to_all.16 = bf16[2,384,768]{2,0,1:T(2,128)(2,1)S(1)} all-to-all(bf16[2,384,768]{2,0,1:T(2,128)(2,1)S(1)} %copy.27), channel_id=1, replica_groups=mesh['pipe'=8,'expert'=4] {'expert'}, dimensions={1} | all-to-all | bytes 2359296 | tf_op jit(solution)/shard_map/all_to_all | solution.py:56
  81.1 1.2 copy.28
  82.2 0.0 all-gather.3.cloned.1.call-update
  82.2 0.2 reduce-scatter.2.cloned.1.call-start
  82.5 110.6 %all-gather.5.cloned.1.call-done = bf16[2,384,6144]{2,1,0:T(8,128)(2,1)} async-done(((bf16[2,384,768]{2,1,0:T(8,128)(2,1)}), bf16[2,384,6144]{2,1,0:T(8,128)(2,1)}) %all-gather.5.cloned.1.call-update) | async-done | bytes 9437200 | tf_op jit(solution)/shard_map/all_gather | solution.py:58
  193.1 16.0 %fusion = f32[2,384,1024]{2,1,0:T(8,128)} fusion(bf16[2,384,6144]{2,1,0:T(8,128)(2,1)} %all-gather.5.cloned.1.call-done, bf16[1,6144,1024]{2,1,0:T(8,128)(2,1)} %param.11), kind=kOutput, calls=%fused_computation.1 | convolution fusion | flops 9663676416 | bytes 25165824 | tf_op jit(solution)/shard_map/wsk,kz->wsz/dot_general | solution.py:62
  209.0 122.1 %all-gather.3.cloned.1.call-done = bf16[2,384,6144]{2,1,0:T(8,128)(2,1)} async-done(((bf16[2,384,768]{2,1,0:T(8,128)(2,1)}), bf16[2,384,6144]{2,1,0:T(8,128)(2,1)}) %all-gather.3.cloned.1.call-update) | async-done | bytes 9437200 | tf_op jit(solution)/shard_map/all_gather | solution.py:59
  331.2 17.7 %multiply_convert_fusion = (bf16[2,384,1024]{2,1,0:T(8,128)(2,1)S(1)}, f32[2,384,1024]{2,1,0:T(8,128)}) fusion(f32[2,384,1024]{2,1,0:T(8,128)} %fusion, bf16[2,384,6144]{2,1,0:T(8,128)(2,1)} %all-gather.3.cloned.1.call-done, bf16[1,1024,6144]{2,1,0:T(8,128)(2,1)} %param.13), kind=kOutput, calls=%fused_computation.12 | convolution fusion | flops 9668395008 | bytes 29884416 | tf_op jit(solution)/shard_map/vun,zn->vuz/dot_general | solution.py:68
  348.9 15.4 %multiply_convert_fusion.1 = bf16[2,384,1024]{2,1,0:T(8,128)(2,1)} fusion(f32[2,384,1024]{2,1,0:T(8,128)} %fusion, f32[2,384,1024]{2,1,0:T(8,128)} %get-tuple-element.7, bf16[2,384,6144]{2,1,0:T(8,128)(2,1)S(1)} %copy-done.5, bf16[1,6144,1024]{2,1,0:T(8,128)(2,1)} %param.12), kind=kOutput, calls=%fused_computation.13 | convolution fusion | flops 9671540736 | bytes 29884416 | tf_op jit(solution)/shard_map/wsk,kz->wsz/dot_general | solution.py:65
  364.3 17.0 %fusion.2 = f32[768,6144]{1,0:T(8,128)} fusion(bf16[768,1024]{1,0:T(8,128)(2,1)} %bitcast.43, bf16[1,6144,1024]{2,1,0:T(8,128)(2,1)} %param.11), kind=kOutput, calls=%fused_computation.3 | convolution fusion | flops 9663676416 | bytes 33030144 | tf_op jit(solution)/shard_map/dot_general | solution.py:21
  381.3 19.4 %fusion.10 = bf16[6144,768]{0,1:T(8,128)(2,1)} fusion(f32[768,6144]{1,0:T(8,128)} %fusion.2, bf16[768,1024]{1,0:T(8,128)(2,1)S(1)} %bitcast.42, bf16[1,6144,1024]{2,1,0:T(8,128)(2,1)} %param.12), kind=kOutput, calls=%fused_computation.11 | convolution fusion | flops 9673113600 | bytes 42467328 | tf_op jit(solution)/shard_map/dot_general | solution.py:21
  400.6 0.0 reduce-scatter.2.cloned.1.call-update
  400.7 161.6 %reduce-scatter.2.cloned.1.call-done = bf16[768,768]{0,1:T(8,128)(2,1)} async-done(((bf16[6144,768]{0,1:T(8,128)(2,1)}), bf16[768,768]{0,1:T(8,128)(2,1)}) %reduce-scatter.2.cloned.1.call-update) | async-done | bytes 1179664 | tf_op jit(solution)/shard_map/reduce_scatter | solution.py:81
  562.3 2.5 copy.32
  564.8 18.4 %all_to_all.17 = bf16[768,2,384]{0,1,2:T(2,128)(2,1)S(1)} all-to-all(bf16[768,2,384]{0,1,2:T(2,128)(2,1)S(1)} %copy.32), channel_id=1, replica_groups=mesh['pipe'=8,'expert'=4] {'expert'}, dimensions={2} | all-to-all | bytes 2359296 | tf_op jit(solution)/shard_map/all_to_all | solution.py:90
  583.2 0.6 fusion.15
  583.8 0.9 reshape.61
  584.8 2.0 reduce_sum.47
  586.8 0.3 fusion.25
  587.1 6.4 %psum.23 = f32[768]{0:T(1024)} all-reduce(f32[768]{0:T(1024)S(1)} %get-tuple-element.2), channel_id=1, replica_groups=mesh['pipe'=8,'expert'=4] {'expert'}, use_global_device_ids=true, to_apply=%region_10.11 | all-reduce | flops 768 | bytes 6144 | tf_op jit(solution)/shard_map/psum | solution.py:98
  593.5 19.4 %psum.22 = f32[2,128]{1,0:T(2,128)S(1)} all-reduce(f32[2,128]{1,0:T(2,128)S(1)} %get-tuple-element.3), channel_id=1, replica_groups=mesh['pipe'=8,'expert'=4] {'pipe'}, use_global_device_ids=true, to_apply=%region_8.9 | all-reduce | flops 256 | bytes 2048 | tf_op jit(solution)/shard_map/psum | solution.py:94
  612.9 1.1 fusion.22
  (20 shorter events, 0.1 us)
Async XLA Ops:
  7.2 185.9 %all-gather.5.cloned.1.call-start = ((), (), s32[]{:S(2)}) async-start(), calls=%async_computation.5 | async-start | bytes 10616832 | tf_op jit(solution)/shard_map/all_gather | solution.py:58
  39.2 19.8 %copy-start.4 = (f32[2,128,2]{1,2,0:T(2,128)S(1)}, f32[2,128,2]{1,2,0:T(2,128)}, u32[]{:S(2)}) copy-start(f32[2,128,2]{1,2,0:T(2,128)} %param.15) | copy-start | bytes 6148
  39.2 20.1 %copy-start.1 = (bf16[2,128,768]{2,1,0:T(8,128)(2,1)S(1)}, bf16[2,128,768]{2,1,0:T(8,128)(2,1)}, u32[]{:S(2)}) copy-start(bf16[2,128,768]{2,1,0:T(8,128)(2,1)} %param.9) | copy-start | bytes 1179652
  59.0 272.2 %all-gather.3.cloned.1.call-start = ((), (), s32[]{:S(2)}) async-start(), calls=%async_computation.4 | async-start | bytes 10616832 | tf_op jit(solution)/shard_map/all_gather | solution.py:59
  82.2 480.0 %reduce-scatter.2.cloned.1.call-start = ((), (), s32[]{:S(2)}) async-start(), calls=%async_computation.6 | async-start | bytes 10616832 | tf_op jit(solution)/shard_map/reduce_scatter | solution.py:81
  331.2 17.7 %copy-start.5 = (bf16[2,384,6144]{2,1,0:T(8,128)(2,1)S(1)}, bf16[2,384,6144]{2,1,0:T(8,128)(2,1)}, u32[]{:S(2)}) copy-start(bf16[2,384,6144]{2,1,0:T(8,128)(2,1)} %all-gather.5.cloned.1.call-done) | copy-start | bytes 28311556
  583.8 2.9 copy-start
  583.8 2.9 copy-start.3
  584.8 28.1 %copy-start.2 = (bf16[2,128,768]{2,1,0:T(8,128)(2,1)S(1)}, bf16[2,128,768]{2,1,0:T(8,128)(2,1)}, u32[]{:S(2)}) copy-start(bf16[2,128,768]{2,1,0:T(8,128)(2,1)} %param.9) | copy-start | bytes 1179652
Sparse Core Ops, SparseCore 0:
  59.1 133.8 all-gather.4
  195.2 135.9 all-gather.2
  400.8 161.4 reduce-scatter.1
where the time goes:
time: 621 us
  waiting for transfers between devices  394 us (63%)
  blocking collectives  104 us (17%)
  matrix products  87.3 us (14%)
  between operations  14 us (2%)
  local copies, waits for them, and re-layouts  12.1 us (2%)
  other arithmetic  8.36 us (1%)
    reduce_scatter x1, waiting for transfers between devices, body(): lax.psum_scatter((contract_last(gate_weight_rows, flat_a) + contract_last...  162 us
    all_gather x1, waiting for transfers between devices, body(): gradient_slice = lax.all_gather(got_g, 'pipe', axis=2, tiled=True)  122 us
    all_gather x1, waiting for transfers between devices, body(): input_slice = lax.all_gather(got_x, 'pipe', axis=2, tiled=True)  111 us
    dot_general x2, matrix products, contract_last(): lax.dot_general(left, right, (((1,), (1,)), ((), ())), preferred_element_...  36.3 us
    psum x1, blocking collectives, body(): squares = lax.psum(jnp.sum(inputs * inputs, axis=-1), 'pipe')  23.1 us
    psum x1, blocking collectives, body(): inner = lax.psum(jnp.sum(scaled * inputs, axis=-1), 'pipe')  19.4 us
    all_to_all x1, blocking collectives, body(): lax.all_to_all(sent_x, 'expert', split_axis=1, concat_axis=1, tiled=True)  18.6 us
    all_to_all x1, blocking collectives, body(): lax.all_to_all(d_rows, 'expert', split_axis=2, concat_axis=2, tiled=True)  18.4 us
  transfers between devices with their start and end apart: 3, of which 3 were waited for; matrix products, arithmetic and copies ran while one was open for 3% of the time, Pallas kernels for 0%

commit v1 on v0

v1 whole, which is shorter than its diff:
```python
import jax
import jax.numpy as jnp
from jax import lax
from jax.sharding import PartitionSpec as P

eps = 1e-05
CORES = 2


def rows_dot(left, right):
    return lax.dot_general(
        left, right, (((1,), (0,)), ((), ())), preferred_element_type=jnp.float32
    )


def contract_last(left, right):
    return lax.dot_general(
        left, right, (((1,), (1,)), ((), ())), preferred_element_type=jnp.float32
    )


def body(saved, top_grad, norm_gain, w_gate, w_up, w_down, routes, gates):
    n_pipe = lax.axis_size("pipe")
    n_experts = lax.axis_size("expert")
    n_x = n_experts // CORES
    micro, tok, part = saved.shape
    width = part * n_pipe
    wg, wu, wd = w_gate[0], w_up[0], w_down[0]
    expert = lax.axis_index("expert")

    def index(x, core):
        return (x % n_x) * CORES + core

    def across(value, shift):
        pairs = [(index(x + shift, c), index(x, c)) for x in range(n_x) for c in range(CORES)]
        return lax.ppermute(value, "expert", pairs)

    def sibling(value):
        return lax.ppermute(value, "expert", [(i, i ^ 1) for i in range(n_experts)])

    inputs = saved.astype(jnp.float32)
    upstream = top_grad.astype(jnp.float32)

    gained = (inputs * norm_gain).astype(jnp.bfloat16).reshape(micro * tok, part)
    mine = lax.all_gather(gained, "pipe", axis=1, tiled=True)
    grads = top_grad.reshape(micro * tok, part)
    grads = jnp.concatenate([grads] + [across(grads, k) for k in range(1, n_x)], axis=0)
    grads = lax.all_gather(grads, "pipe", axis=1, tiled=True)
    own_x = [mine] + [across(mine, k) for k in range(1, n_x)]
    x_rows = [(value, sibling(value)) for value in own_x]
    g_rows = (grads, sibling(grads))

    squares = lax.psum(jnp.sum(inputs * inputs, axis=-1), "pipe")
    scale = lax.rsqrt(squares / width + eps)
    facts = jnp.concatenate(
        [scale[None], jnp.moveaxis(gates, 2, 0), jnp.moveaxis(routes, 2, 0).astype(jnp.float32)],
        axis=0,
    ).reshape(5, micro * tok)
    facts = lax.all_gather(facts, "expert", axis=0)
    chip, core = expert // CORES, expert % CORES
    named = expert.astype(jnp.float32)

    def block_facts(k, flip):
        source = ((chip + k) % n_x) * CORES + jnp.where(flip, 1 - core, core)
        block = lax.dynamic_index_in_dim(facts, source, 0, keepdims=False)
        gate = jnp.where(block[3] == named, block[1], 0.0) + jnp.where(
            block[4] == named, block[2], 0.0
        )
        return block[0][:, None], gate[:, None]

    span = micro * tok
    hidden_grads = {}
    for flip in range(CORES):
        d_hidden_all = contract_last(g_rows[flip], wd)
        for k in range(n_x):
            row_scale, row_gate = block_facts(k, flip)
            pre_a = rows_dot(x_rows[k][flip], wg) * row_scale
            pre_b = rows_dot(x_rows[k][flip], wu) * row_scale
            d_hidden = d_hidden_all[k * span : (k + 1) * span] * row_gate
            sig = jax.nn.sigmoid(pre_a)
            d_a = (d_hidden * pre_b * sig * (1.0 + pre_a * (1.0 - sig))).astype(jnp.bfloat16)
            d_b = (d_hidden * (pre_a * sig)).astype(jnp.bfloat16)
            hidden_grads[flip, k] = (d_a, d_b)

    def back(flip, m):
        pieces = [
            tuple(v[m * tok : (m + 1) * tok] for v in hidden_grads[flip, k]) for k in range(n_x)
        ]
        left = jnp.concatenate([a for a, b in pieces], axis=0)
        right = jnp.concatenate([b for a, b in pieces], axis=0)
        return contract_last(wg, left) + contract_last(wu, right)

    def scatter(value):
        return lax.psum_scatter(value, "pipe", scatter_dimension=0, tiled=True)

    others = [sibling(back(1, m).astype(jnp.bfloat16)) for m in reversed(range(micro))][::-1]
    norms = [None] * micro
    for m in reversed(range(micro)):
        chip_sum = back(0, m) + others[m].astype(jnp.float32)
        if m == 0 and micro > 1:
            total = chip_sum[:, :tok]
            for k in range(1, n_x):
                piece = chip_sum[:, k * tok : (k + 1) * tok].astype(jnp.bfloat16)
                total = total + across(piece, n_x - k).astype(jnp.float32)
            norms[m] = scatter(total.astype(jnp.bfloat16)).astype(jnp.float32)
        else:
            reduced = scatter(chip_sum.astype(jnp.bfloat16))
            total = reduced[:, :tok].astype(jnp.float32)
            for k in range(1, n_x):
                total = total + across(reduced[:, k * tok : (k + 1) * tok], n_x - k).astype(
                    jnp.float32
                )
            norms[m] = total
    d_norm = jnp.stack([value.T for value in norms], axis=0)
    scale = scale[:, :, None]
    scaled = norm_gain * d_norm
    inner = lax.psum(jnp.sum(scaled * inputs, axis=-1), "pipe")
    d_x = scale * scaled - inputs * scale**3 * (inner / width)[:, :, None]
    input_grads = upstream + d_x
    gain_part = jnp.sum(d_norm * inputs * scale, axis=(0, 1))
    grad_gain = lax.psum(gain_part, "expert")
    return (input_grads, grad_gain)


def solution(mesh):
    placed = (
        P(None, "expert", "pipe"),
        P(None, "expert", "pipe"),
        P("pipe"),
        P("expert", None, "pipe"),
        P("expert", None, "pipe"),
        P("expert", "pipe", None),
        P(None, "expert", None),
        P(None, "expert", None),
    )
    return jax.shard_map(
        body,
        mesh=mesh,
        in_specs=placed,
        out_specs=(P(None, "expert", "pipe"), P("pipe")),
        check_vma=False,
    )
```

time: 621 us -> 515 us (0.83)
  waiting for transfers between devices: 394 us -> 186 us
  matrix products: 87.3 us -> 191 us
  blocking collectives: 104 us -> 92.3 us
  starting transfers between devices: 0.3 us -> 9.1 us
  local copies, waits for them, and re-layouts: 12.1 us -> 5.72 us
    all_gather x2, waiting for transfers between devices: 233 us -> 69.9 us  [the longest x1 49.9 us: body(): mine = lax.all_gather(gained, 'pipe', axis=1, tiled=True)]
    dot_general x2 -> x10, matrix products: 36.3 us -> 135 us  [contract_last(): lax.dot_general(left, right, (((1,), (1,)), ((), ())), preferred_element_...]
    reduce_scatter x1 -> x2, waiting for transfers between devices: 162 us -> 70.9 us  [scatter(): return lax.psum_scatter(value, 'pipe', scatter_dimension=0, tiled=True)]
    all_to_all x3 -> x0, blocking collectives: 55.3 us -> none  [the longest x1 18.6 us: body(): lax.all_to_all(sent_x, 'expert', split_axis=1, concat_axis=1, tiled=True)]
    all_gather x0 -> x1, blocking collectives: none -> 47.2 us  [body(): facts = lax.all_gather(facts, 'expert', axis=0)]
    ppermute x0 -> x9, waiting for transfers between devices: none -> 44.7 us  [the longest x4 44.7 us: across(): return lax.ppermute(value, 'expert', pairs)]
    ppermute x0 -> x9, starting transfers between devices: none -> 8.64 us  [the longest x4 7.55 us: across(): return lax.ppermute(value, 'expert', pairs)]
    dot_general x6 -> x8, matrix products: 51 us -> 56.5 us  [rows_dot(): lax.dot_general(left, right, (((1,), (0,)), ((), ())), preferred_element_...]
  transfers between devices with their start and end apart: 3 -> 13, of which waited for: 3 -> 6; matrix products, arithmetic and copies ran while one was open for 3% -> 32% of each run, Pallas kernels for 0% -> 0%
where the time goes in v1:
time: 515 us; the launch traced here: 511 us
  matrix products  191 us (37%)
  waiting for transfers between devices  186 us (36%)
  blocking collectives  92.3 us (18%)
  between operations  14.5 us (3%)
  other arithmetic  12.6 us (2%)
  starting transfers between devices  9.1 us (2%)
  local copies, waits for them, and re-layouts  5.72 us (1%)
    dot_general x10, matrix products, contract_last(): lax.dot_general(left, right, (((1,), (1,)), ((), ())), preferred_element_...  135 us
    reduce_scatter x2, waiting for transfers between devices, scatter(): return lax.psum_scatter(value, 'pipe', scatter_dimension=0, tiled=True)  70.9 us
    dot_general x8, matrix products, rows_dot(): lax.dot_general(left, right, (((1,), (0,)), ((), ())), preferred_element_...  56.5 us
    all_gather x1, waiting for transfers between devices, body(): mine = lax.all_gather(gained, 'pipe', axis=1, tiled=True)  49.9 us
    all_gather x1, blocking collectives, body(): facts = lax.all_gather(facts, 'expert', axis=0)  47.2 us
    ppermute x4, waiting for transfers between devices, across(): return lax.ppermute(value, 'expert', pairs)  44.7 us
    all_gather x1, waiting for transfers between devices, body(): grads = lax.all_gather(grads, 'pipe', axis=1, tiled=True)  20 us
    psum x1, blocking collectives, body(): squares = lax.psum(jnp.sum(inputs * inputs, axis=-1), 'pipe')  19.4 us
  transfers between devices with their start and end apart: 13, of which 6 were waited for; matrix products, arithmetic and copies ran while one was open for 32% of the time, Pallas kernels for 0%

profile of v1, /device:TPU:0, one launch (start us, length us, event | category | flops | bytes accessed | tf_op | source)
XLA Modules:
  0.0 511.1 jit_solution(9122861197693901689)
XLA Ops:
  7.2 1.9 fusion.139
  9.2 3.0 collective-permute-start
  12.2 9.3 %collective-permute-done = bf16[256,768]{1,0:T(8,128)(2,1)S(1)} collective-permute-done((bf16[256,768]{1,0:T(8,128)(2,1)}, bf16[256,768]{1,0:T(8,128)(2,1)S(1)}, u32[]{:S(2)}, u32[]{:S(2)}) %collective-permute-start) | collective-permute-done | bytes 393248 | tf_op jit(solution)/shard_map/ppermute | solution.py:36
  21.5 1.9 pad_maximum_fusion
  23.5 49.9 %all-gather.5.cloned.1.call-done = bf16[256,6144]{1,0:T(8,128)(2,1)} async-done(((bf16[256,768]{1,0:T(8,128)(2,1)}), bf16[256,6144]{1,0:T(8,128)(2,1)}) %all-gather.5.cloned.1.call-update) | async-done | bytes 3145744 | tf_op jit(solution)/shard_map/all_gather | solution.py:45
  73.4 1.5 collective-permute-start.1
  74.9 19.4 %psum.21 = f32[2,128]{1,0:T(2,128)S(1)} all-reduce(f32[2,128]{1,0:T(2,128)S(1)} %get-tuple-element.24), channel_id=1, replica_groups=mesh['pipe'=8,'expert'=4] {'pipe'}, use_global_device_ids=true, to_apply=%region_1.0 | all-reduce | flops 256 | bytes 2048 | tf_op jit(solution)/shard_map/psum | solution.py:53
  94.3 0.5 multiply_multiply_fusion
  94.9 0.7 convert_bitcast_fusion.1
  95.5 0.7 pad_maximum_fusion.2
  96.2 47.2 %all_gather.10 = f32[4,5,256]{2,1,0:T(8,128)S(1)} all-gather(f32[1,5,256]{2,1,0:T(8,128)S(1)} %pad_maximum_fusion.2), channel_id=1, replica_groups=mesh['pipe'=8,'expert'=4] {'expert'}, dimensions={0}, use_global_device_ids=true | all-gather | bytes 25600 | tf_op jit(solution)/shard_map/all_gather | solution.py:59
  143.5 0.4 collective-permute-start.3
  144.0 10.0 %fusion.82 = f32[256,1024]{1,0:T(8,128)} fusion(bf16[256,6144]{1,0:T(8,128)(2,1)} %collective-permute-done.1, bf16[1,6144,1024]{2,1,0:T(8,128)(2,1)} %param.11, f32[256]{0:T(256)S(1)} %bitcast.184), kind=kOutput, calls=%fused_computation.61 | convolution fusion | flops 3221487616 | bytes 16778240 | tf_op jit(solution)/shard_map/dot_general | solution.py:11
  154.1 20.0 %all-gather.3.cloned.1.call-done = bf16[512,6144]{1,0:T(8,128)(2,1)} async-done(((bf16[512,768]{1,0:T(8,128)(2,1)}), bf16[512,6144]{1,0:T(8,128)(2,1)}) %all-gather.3.cloned.1.call-update) | async-done | bytes 6291472 | tf_op jit(solution)/shard_map/all_gather | solution.py:48
  174.0 12.0 %fusion.34 = f32[512,1024]{1,0:T(8,128)S(1)} fusion(bf16[512,6144]{1,0:T(8,128)(2,1)} %all-gather.3.cloned.1.call-done, bf16[1,1024,6144]{2,1,0:T(8,128)(2,1)} %param.13), kind=kOutput, calls=%fused_computation.34 | convolution fusion | flops 6442450944 | bytes 20971520 | tf_op jit(solution)/shard_map/dot_general | solution.py:17
  186.1 9.3 %fusion.133 = bf16[256,1024]{1,0:T(8,128)(2,1)S(1)} fusion(bf16[256,6144]{1,0:T(8,128)(2,1)} %collective-permute-done.1, bf16[1,6144,1024]{2,1,0:T(8,128)(2,1)} %param.12, f32[256,1024]{1,0:T(8,128)S(1)} %copy-done.7, f32[512,1024]{1,0:T(8,128)S(1)} %fusion.34, f32[256]{0:T(256)S(1)} %bitcast.185, f32[256]{0:T(256)S(1)} %bitcast.182), kind=kOutput, calls=%fused_computation.78 | convolution fusion | flops 3224371200 | bytes 18352128 | tf_op jit(solution)/shard_map/dot_general | solution.py:11
  195.5 0.7 fusion.194
  196.2 6.9 %multiply_convert_fusion.3 = (bf16[256,1024]{1,0:T(8,128)(2,1)S(1)}, bf16[256,1024]{1,0:T(8,128)(2,1)S(1)}, f32[256,1024]{1,0:T(8,128)S(1)}) fusion(f32[512,1024]{1,0:T(8,128)S(1)} %fusion.34, f32[256]{0:T(256)S(1)} %bitcast.178, f32[256,1024]{1,0:T(8,128)S(1)} %copy-done.8, f32[256]{0:T(256)S(1)} %bitcast.183, f32[256]{0:T(256)S(1)} %bitcast.180, ...), kind=kOutput, calls=%fused_computation.89 | convolution fusion | flops 3225157632 | bytes 20974592 | tf_op jit(solution)/shard_map/dot_general | solution.py:11
  203.2 3.8 fusion.136
  207.0 0.8 fusion.193
  207.7 0.9 fusion.191
  208.7 7.3 %fusion.88 = f32[256,1024]{1,0:T(8,128)S(1)} fusion(bf16[256,6144]{1,0:T(8,128)(2,1)} %collective-permute-done.4, bf16[1,6144,1024]{2,1,0:T(8,128)(2,1)} %param.11, f32[256]{0:T(256)S(1)} %bitcast.176), kind=kOutput, calls=%fused_computation.63 | convolution fusion | flops 3221487616 | bytes 16778240 | tf_op jit(solution)/shard_map/dot_general | solution.py:11
  216.0 11.7 %fusion.32 = f32[512,1024]{1,0:T(8,128)S(1)} fusion(bf16[512,6144]{1,0:T(8,128)(2,1)} %collective-permute-done.2, bf16[1,1024,6144]{2,1,0:T(8,128)(2,1)} %param.13), kind=kOutput, calls=%fused_computation.32 | convolution fusion | flops 6442450944 | bytes 20971520 | tf_op jit(solution)/shard_map/dot_general | solution.py:17
  227.7 5.7 %fusion.127 = bf16[256,1024]{1,0:T(8,128)(2,1)S(1)} fusion(bf16[256,6144]{1,0:T(8,128)(2,1)} %collective-permute-done.4, bf16[1,6144,1024]{2,1,0:T(8,128)(2,1)S(1)} %bitcast.164, f32[256,1024]{1,0:T(8,128)S(1)} %fusion.88, f32[512,1024]{1,0:T(8,128)S(1)} %fusion.32, f32[256]{0:T(256)S(1)} %bitcast.177, f32[256]{0:T(256)S(1)} %bitcast.174), kind=kOutput, calls=%fused_computation.76 | convolution fusion | flops 3224371200 | bytes 18352128 | tf_op jit(solution)/shard_map/dot_general | solution.py:11
  233.4 7.7 %multiply_convert_fusion.1 = (bf16[256,1024]{1,0:T(8,128)(2,1)S(1)}, bf16[256,1024]{1,0:T(8,128)(2,1)S(1)}, f32[256,1024]{1,0:T(8,128)S(1)}) fusion(f32[512,1024]{1,0:T(8,128)S(1)} %fusion.32, f32[256]{0:T(256)S(1)} %bitcast.170, f32[256,1024]{1,0:T(8,128)S(1)} %fusion.88, f32[256]{0:T(256)S(1)} %bitcast.175, f32[256]{0:T(256)S(1)} %bitcast.172, ...), kind=kOutput, calls=%fused_computation.85 | convolution fusion | flops 3225157632 | bytes 20974592 | tf_op jit(solution)/shard_map/dot_general | solution.py:11
  241.2 5.7 %fusion.130 = bf16[256,1024]{1,0:T(8,128)(2,1)S(1)} fusion(bf16[256,6144]{1,0:T(8,128)(2,1)} %collective-permute-done.3, bf16[1,6144,1024]{2,1,0:T(8,128)(2,1)S(1)} %bitcast.164, f32[256,1024]{1,0:T(8,128)S(1)} %get-tuple-element.36, f32[512,1024]{1,0:T(8,128)S(1)} %fusion.32, f32[256]{0:T(256)S(1)} %bitcast.173, f32[256]{0:T(256)S(1)} %bitcast.171), kind=kOutput, calls=%fused_computation.77 | convolution fusion | flops 3224371200 | bytes 18352128 | tf_op jit(solution)/shard_map/dot_general | solution.py:11
  246.9 14.9 %fusion = f32[256,6144]{1,0:T(8,128)} fusion(bf16[1,6144,1024]{2,1,0:T(8,128)(2,1)} %param.11, bf16[128,1024]{1,0:T(8,128)(2,1)S(1)} %get-tuple-element.23, bf16[128,1024]{1,0:T(8,128)(2,1)S(1)} %get-tuple-element.21), kind=kOutput, calls=%fused_computation | convolution fusion | flops 3222274048 | bytes 19398656 | tf_op jit(solution)/shard_map/dot_general | solution.py:17
  261.9 15.2 %fusion.63 = bf16[6144,256]{0,1:T(8,128)(2,1)} fusion(f32[256,6144]{1,0:T(8,128)} %fusion, bf16[1,6144,1024]{2,1,0:T(8,128)(2,1)} %param.12, bf16[128,1024]{1,0:T(8,128)(2,1)S(1)} %get-tuple-element.38, bf16[128,1024]{1,0:T(8,128)(2,1)S(1)} %get-tuple-element.17), kind=kOutput, calls=%fused_computation.45 | convolution fusion | flops 3225419776 | bytes 22544384 | tf_op jit(solution)/shard_map/dot_general | solution.py:17
  277.1 0.5 collective-permute-start.7
  277.6 14.7 %fusion.2 = f32[256,6144]{1,0:T(8,128)} fusion(bf16[1,6144,1024]{2,1,0:T(8,128)(2,1)} %param.11, bf16[128,1024]{1,0:T(8,128)(2,1)S(1)} %get-tuple-element.15, bf16[128,1024]{1,0:T(8,128)(2,1)S(1)} %get-tuple-element.13), kind=kOutput, calls=%fused_computation.2 | convolution fusion | flops 3222274048 | bytes 19398656 | tf_op jit(solution)/shard_map/dot_general | solution.py:17
  292.3 14.7 %fusion.4 = f32[256,6144]{1,0:T(8,128)} fusion(bf16[1,6144,1024]{2,1,0:T(8,128)(2,1)} %param.11, bf16[128,1024]{1,0:T(8,128)(2,1)S(1)} %get-tuple-element.22, bf16[128,1024]{1,0:T(8,128)(2,1)S(1)} %get-tuple-element.20), kind=kOutput, calls=%fused_computation.4 | convolution fusion | flops 3222274048 | bytes 19398656 | tf_op jit(solution)/shard_map/dot_general | solution.py:17
  307.0 15.4 %fusion.60 = bf16[6144,256]{0,1:T(8,128)(2,1)} fusion(f32[256,6144]{1,0:T(8,128)} %fusion.4, bf16[1,6144,1024]{2,1,0:T(8,128)(2,1)} %param.12, bf16[128,1024]{1,0:T(8,128)(2,1)S(1)} %get-tuple-element.39, bf16[128,1024]{1,0:T(8,128)(2,1)S(1)} %get-tuple-element.16), kind=kOutput, calls=%fused_computation.44 | convolution fusion | flops 3225419776 | bytes 22544384 | tf_op jit(solution)/shard_map/dot_general | solution.py:17
  322.4 12.7 %add_convert_fusion = bf16[6144,256]{0,1:T(8,128)(2,1)} fusion(bf16[6144,256]{0,1:T(8,128)(2,1)} %collective-permute-done.7, f32[256,6144]{1,0:T(8,128)} %fusion.2, bf16[1,6144,1024]{2,1,0:T(8,128)(2,1)} %param.12, bf16[128,1024]{1,0:T(8,128)(2,1)} %get-tuple-element.40, bf16[128,1024]{1,0:T(8,128)(2,1)} %get-tuple-element.9), kind=kOutput, calls=%fused_computation.46 | convolution fusion | flops 3228565504 | bytes 25690112 | tf_op jit(solution)/shard_map/dot_general | solution.py:17
  335.4 10.9 %fusion.10 = f32[256,6144]{1,0:T(8,128)} fusion(bf16[1,6144,1024]{2,1,0:T(8,128)(2,1)} %param.11, bf16[128,1024]{1,0:T(8,128)(2,1)} %get-tuple-element.14, bf16[128,1024]{1,0:T(8,128)(2,1)} %get-tuple-element.12), kind=kOutput, calls=%fused_computation.10 | convolution fusion | flops 3222274048 | bytes 19398656 | tf_op jit(solution)/shard_map/dot_general | solution.py:17
  346.3 12.7 %convert_add_fusion = f32[6144,256]{0,1:T(8,128)} fusion(bf16[6144,256]{0,1:T(8,128)(2,1)S(1)} %collective-permute-done.5, f32[256,6144]{1,0:T(8,128)} %fusion.10, bf16[1,6144,1024]{2,1,0:T(8,128)(2,1)} %param.12, bf16[128,1024]{1,0:T(8,128)(2,1)} %get-tuple-element.41, bf16[128,1024]{1,0:T(8,128)(2,1)S(1)} %get-tuple-element.8), kind=kOutput, calls=%fused_computation.47 | convolution fusion | flops 3226992640 | bytes 28835840 | tf_op jit(solution)/shard_map/dot_general | solution.py:17
  359.1 2.2 slice.246
  361.2 1.5 collective-permute-start.6
  362.8 35.3 %collective-permute-done.6 = bf16[6144,128]{0,1:T(8,128)(2,1)S(1)} collective-permute-done((bf16[6144,128]{0,1:T(8,128)(2,1)S(1)}, bf16[6144,128]{0,1:T(8,128)(2,1)S(1)}, u32[]{:S(2)}, u32[]{:S(2)}) %collective-permute-start.6) | collective-permute-done | bytes 1572896 | tf_op jit(solution)/shard_map/ppermute | solution.py:36
  398.1 3.4 fusion.66
  401.6 6.2 %reduce-scatter.5.cloned.1.call-done = bf16[768,256]{0,1:T(8,128)(2,1)} async-done(((bf16[6144,256]{0,1:T(8,128)(2,1)}), bf16[768,256]{0,1:T(8,128)(2,1)}) %reduce-scatter.5.cloned.1.call-update) | async-done | bytes 393232 | tf_op jit(solution)/shard_map/reduce_scatter | solution.py:94
  407.8 0.9 slice.220
  408.7 1.5 collective-permute-start.8
  410.3 64.7 %reduce-scatter.3.cloned.1.call-done = bf16[768,128]{0,1:T(8,128)(2,1)} async-done(((bf16[6144,128]{0,1:T(8,128)(2,1)}), bf16[768,128]{0,1:T(8,128)(2,1)}) %reduce-scatter.3.cloned.1.call-update) | async-done | bytes 196624 | tf_op jit(solution)/shard_map/reduce_scatter | solution.py:94
  475.0 1.0 convert_bitcast_fusion
  475.9 1.0 add_bitcast_fusion
  477.3 19.4 %psum.22 = f32[2,128]{1,0:T(2,128)S(1)} all-reduce(f32[2,128]{1,0:T(2,128)S(1)} %get-tuple-element.3), channel_id=1, replica_groups=mesh['pipe'=8,'expert'=4] {'pipe'}, use_global_device_ids=true, to_apply=%region_5.6 | all-reduce | flops 256 | bytes 2048 | tf_op jit(solution)/shard_map/psum | solution.py:117
  496.7 6.2 %psum.23 = f32[768]{0:T(1024)} all-reduce(f32[768]{0:T(1024)S(1)} %get-tuple-element.2), channel_id=1, replica_groups=mesh['pipe'=8,'expert'=4] {'expert'}, use_global_device_ids=true, to_apply=%region_7.8 | all-reduce | flops 768 | bytes 6144 | tf_op jit(solution)/shard_map/psum | solution.py:121
  502.9 1.1 fusion.143
  (49 shorter events, 1.3 us)
Async XLA Ops:
  7.2 66.3 %all-gather.5.cloned.1.call-start = ((), (), s32[]{:S(2)}) async-start(), calls=%async_computation.3 | async-start | bytes 3538944 | tf_op jit(solution)/shard_map/all_gather | solution.py:45
  9.1 164.9 %all-gather.3.cloned.1.call-start = ((), (), s32[]{:S(2)}) async-start(), calls=%async_computation.2 | async-start | bytes 7077888 | tf_op jit(solution)/shard_map/all_gather | solution.py:48
  9.2 12.3 %collective-permute-start = (bf16[256,768]{1,0:T(8,128)(2,1)}, bf16[256,768]{1,0:T(8,128)(2,1)S(1)}, u32[]{:S(2)}, u32[]{:S(2)}) collective-permute-start(bf16[256,768]{1,0:T(8,128)(2,1)} %bitcast.165), channel_id=1, source_target_pairs={{2,0},{3,1},{0,2},{1,3},{6,4},{7,5},{4,6},{5,7},{10,8},{11,9},{8,1... | collective-permute-start | bytes 1179656 | tf_op jit(solution)/shard_map/ppermute | solution.py:36
  23.5 384.3 %reduce-scatter.5.cloned.1.call-start = ((), (), s32[]{:S(2)}) async-start(), calls=%async_computation.5 | async-start | bytes 3538944 | tf_op jit(solution)/shard_map/reduce_scatter | solution.py:94
  73.4 70.4 %collective-permute-start.1 = (bf16[256,6144]{1,0:T(8,128)(2,1)}, bf16[256,6144]{1,0:T(8,128)(2,1)}, u32[]{:S(2)}, u32[]{:S(2)}) collective-permute-start(bf16[256,6144]{1,0:T(8,128)(2,1)} %all-gather.5.cloned.1.call-done), channel_id=1, source_target_pairs={{2,0},{3,1},{0,2},{1,3},{6,4},{7,5},{4,6},{5,7},{10,8},{11,9},{8,1... | collective-permute-start | bytes 9437192 | tf_op jit(solution)/shard_map/ppermute | solution.py:36
  94.9 0.7 copy-start.3
  143.5 90.0 %collective-permute-start.3 = (bf16[256,6144]{1,0:T(8,128)(2,1)}, bf16[256,6144]{1,0:T(8,128)(2,1)}, u32[]{:S(2)}, u32[]{:S(2)}) collective-permute-start(bf16[256,6144]{1,0:T(8,128)(2,1)} %all-gather.5.cloned.1.call-done), channel_id=1, source_target_pairs={{0,1},{1,0},{2,3},{3,2},{4,5},{5,4},{6,7},{7,6},{8,9},{9,8},{10,11... | collective-permute-start | bytes 9437192 | tf_op jit(solution)/shard_map/ppermute | solution.py:39
  143.8 64.8 %collective-permute-start.4 = (bf16[256,6144]{1,0:T(8,128)(2,1)}, bf16[256,6144]{1,0:T(8,128)(2,1)}, u32[]{:S(2)}, u32[]{:S(2)}) collective-permute-start(bf16[256,6144]{1,0:T(8,128)(2,1)} %collective-permute-done.1), channel_id=1, source_target_pairs={{0,1},{1,0},{2,3},{3,2},{4,5},{5,4},{6,7},{7,6},{8,9},{9,8},{10,11... | collective-permute-start | bytes 9437192 | tf_op jit(solution)/shard_map/ppermute | solution.py:39
  174.0 12.0 %copy-start.7 = (f32[256,1024]{1,0:T(8,128)S(1)}, f32[256,1024]{1,0:T(8,128)}, u32[]{:S(2)}) copy-start(f32[256,1024]{1,0:T(8,128)} %fusion.82) | copy-start | bytes 3145732
  174.0 42.0 %collective-permute-start.2 = (bf16[512,6144]{1,0:T(8,128)(2,1)}, bf16[512,6144]{1,0:T(8,128)(2,1)}, u32[]{:S(2)}, u32[]{:S(2)}) collective-permute-start(bf16[512,6144]{1,0:T(8,128)(2,1)} %all-gather.3.cloned.1.call-done), channel_id=1, source_target_pairs={{0,1},{1,0},{2,3},{3,2},{4,5},{5,4},{6,7},{7,6},{8,9},{9,8},{10,11... | collective-permute-start | bytes 18874376 | tf_op jit(solution)/shard_map/ppermute | solution.py:39
  186.1 10.1 %copy-start.6 = (bf16[256,6144]{1,0:T(8,128)(2,1)S(1)}, bf16[256,6144]{1,0:T(8,128)(2,1)}, u32[]{:S(2)}) copy-start(bf16[256,6144]{1,0:T(8,128)(2,1)} %all-gather.5.cloned.1.call-done) | copy-start | bytes 9437188
  186.1 10.1 %copy-start.8 = (f32[256,1024]{1,0:T(8,128)S(1)}, f32[256,1024]{1,0:T(8,128)}, u32[]{:S(2)}) copy-start(f32[256,1024]{1,0:T(8,128)} %fusion.82) | copy-start | bytes 3145732
  186.1 17.1 %slice-start = ((s8[12582912]{0:T(1024)(128)(4,1)}), s8[4194304]{0:T(1024)(128)(4,1)S(1)}, s32[]{:S(2)}) async-start(s8[12582912]{0:T(1024)(128)(4,1)} %bitcast.163), calls=%async_computation.6 | async-start | bytes 8388608
  186.1 17.1 %slice-start.1 = ((s8[12582912]{0:T(1024)(128)(4,1)}), s8[4194304]{0:T(1024)(128)(4,1)S(1)}, s32[]{:S(2)}) async-start(s8[12582912]{0:T(1024)(128)(4,1)} %bitcast.163), calls=%async_computation.7 | async-start | bytes 8388608
  196.2 7.0 %slice-start.2 = ((s8[12582912]{0:T(1024)(128)(4,1)}), s8[4194304]{0:T(1024)(128)(4,1)S(1)}, s32[]{:S(2)}) async-start(s8[12582912]{0:T(1024)(128)(4,1)} %bitcast.163), calls=%async_computation.8 | async-start | bytes 8388608
  277.1 45.2 %collective-permute-start.7 = (bf16[6144,256]{0,1:T(8,128)(2,1)}, bf16[6144,256]{0,1:T(8,128)(2,1)}, u32[]{:S(2)}, u32[]{:S(2)}) collective-permute-start(bf16[6144,256]{0,1:T(8,128)(2,1)} %fusion.63), channel_id=1, source_target_pairs={{0,1},{1,0},{2,3},{3,2},{4,5},{5,4},{6,7},{7,6},{8,9},{9,8},{10,11... | collective-permute-start | bytes 9437192 | tf_op jit(solution)/shard_map/ppermute | solution.py:39
  322.4 23.9 %collective-permute-start.5 = (bf16[6144,256]{0,1:T(8,128)(2,1)}, bf16[6144,256]{0,1:T(8,128)(2,1)S(1)}, u32[]{:S(2)}, u32[]{:S(2)}) collective-permute-start(bf16[6144,256]{0,1:T(8,128)(2,1)} %fusion.60), channel_id=1, source_target_pairs={{0,1},{1,0},{2,3},{3,2},{4,5},{5,4},{6,7},{7,6},{8,9},{9,8},{10,11... | collective-permute-start | bytes 9437192 | tf_op jit(solution)/shard_map/ppermute | solution.py:39
  335.1 139.9 %reduce-scatter.3.cloned.1.call-start = ((), (), s32[]{:S(2)}) async-start(), calls=%async_computation.4 | async-start | bytes 1769472 | tf_op jit(solution)/shard_map/reduce_scatter | solution.py:94
  359.0 117.9 %copy-start = (bf16[2,128,768]{2,1,0:T(8,128)(2,1)S(1)}, bf16[2,128,768]{2,1,0:T(8,128)(2,1)}, u32[]{:S(2)}) copy-start(bf16[2,128,768]{2,1,0:T(8,128)(2,1)} %param.8) | copy-start | bytes 1179652
  359.0 117.9 %copy-start.2 = (f32[768]{0:T(1024)S(1)}, f32[768]{0:T(1024)}, u32[]{:S(2)}) copy-start(f32[768]{0:T(1024)} %param.10) | copy-start | bytes 9220
  359.0 117.9 %copy-start.4 = (f32[2,128]{1,0:T(2,128)S(1)}, f32[2,128]{1,0:T(2,128)}, u32[]{:S(2)}) copy-start(f32[2,128]{1,0:T(2,128)} %copy-done.3) | copy-start | bytes 3076
  359.0 143.9 %copy-start.1 = (bf16[2,128,768]{2,1,0:T(8,128)(2,1)S(1)}, bf16[2,128,768]{2,1,0:T(8,128)(2,1)}, u32[]{:S(2)}) copy-start(bf16[2,128,768]{2,1,0:T(8,128)(2,1)} %param.9) | copy-start | bytes 1179652
  359.1 143.9 %copy-start.5 = (f32[2,128]{1,0:T(2,128)S(1)}, f32[2,128]{1,0:T(2,128)}, u32[]{:S(2)}) copy-start(f32[2,128]{1,0:T(2,128)} %get-tuple-element.34) | copy-start | bytes 3076
  361.2 36.9 %collective-permute-start.6 = (bf16[6144,128]{0,1:T(8,128)(2,1)S(1)}, bf16[6144,128]{0,1:T(8,128)(2,1)S(1)}, u32[]{:S(2)}, u32[]{:S(2)}) collective-permute-start(bf16[6144,128]{0,1:T(8,128)(2,1)S(1)} %slice.246), channel_id=1, source_target_pairs={{2,0},{3,1},{0,2},{1,3},{6,4},{7,5},{4,6},{5,7},{10,8},{11,9},{8,1... | collective-permute-start | bytes 4718600 | tf_op jit(solution)/shard_map/ppermute | solution.py:36
  408.7 67.2 %collective-permute-start.8 = (bf16[768,128]{0,1:T(8,128)(2,1)S(1)}, bf16[768,128]{0,1:T(8,128)(2,1)S(1)}, u32[]{:S(2)}, u32[]{:S(2)}) collective-permute-start(bf16[768,128]{0,1:T(8,128)(2,1)S(1)} %slice.220), channel_id=1, source_target_pairs={{2,0},{3,1},{0,2},{1,3},{6,4},{7,5},{4,6},{5,7},{10,8},{11,9},{8,1... | collective-permute-start | bytes 589832 | tf_op jit(solution)/shard_map/ppermute | solution.py:36
Sparse Core Ops, SparseCore 0:
  10.2 63.1 all-gather.4
  76.2 97.7 all-gather.2
  335.2 72.5 reduce-scatter.4
  411.1 63.8 reduce-scatter.2

commit v2 on v1

--- a/solution.py
+++ b/solution.py
@@ -46,10 +46,6 @@
     grads = top_grad.reshape(micro * tok, part)
     grads = jnp.concatenate([grads] + [across(grads, k) for k in range(1, n_x)], axis=0)
     grads = lax.all_gather(grads, "pipe", axis=1, tiled=True)
-    own_x = [mine] + [across(mine, k) for k in range(1, n_x)]
-    x_rows = [(value, sibling(value)) for value in own_x]
-    g_rows = (grads, sibling(grads))
-
     squares = lax.psum(jnp.sum(inputs * inputs, axis=-1), "pipe")
     scale = lax.rsqrt(squares / width + eps)
     facts = jnp.concatenate(
@@ -57,6 +53,9 @@
         axis=0,
     ).reshape(5, micro * tok)
     facts = lax.all_gather(facts, "expert", axis=0)
+    mine, facts = lax.optimization_barrier((mine, facts))
+    own_x = [mine] + [across(mine, k) for k in range(1, n_x)]
+    x_rows = [(value, sibling(value)) for value in own_x]
     chip, core = expert // CORES, expert % CORES
     named = expert.astype(jnp.float32)
 
@@ -69,34 +68,44 @@
         return block[0][:, None], gate[:, None]
 
     span = micro * tok
+    pieces = [(flip, k) for flip in range(CORES) for k in range(n_x)]
+    gate_pre = [rows_dot(x_rows[k][flip], wg) for flip, k in pieces]
+    up_pre = [rows_dot(x_rows[k][flip], wu) for flip, k in pieces]
+    grads, gate_pre, up_pre = lax.optimization_barrier((grads, gate_pre, up_pre))
+    g_rows = (grads, sibling(grads))
+    d_hidden_all = [contract_last(rows, wd) for rows in g_rows]
     hidden_grads = {}
-    for flip in range(CORES):
-        d_hidden_all = contract_last(g_rows[flip], wd)
-        for k in range(n_x):
-            row_scale, row_gate = block_facts(k, flip)
-            pre_a = rows_dot(x_rows[k][flip], wg) * row_scale
-            pre_b = rows_dot(x_rows[k][flip], wu) * row_scale
-            d_hidden = d_hidden_all[k * span : (k + 1) * span] * row_gate
-            sig = jax.nn.sigmoid(pre_a)
-            d_a = (d_hidden * pre_b * sig * (1.0 + pre_a * (1.0 - sig))).astype(jnp.bfloat16)
-            d_b = (d_hidden * (pre_a * sig)).astype(jnp.bfloat16)
-            hidden_grads[flip, k] = (d_a, d_b)
+    for (flip, k), pre_a, pre_b in zip(pieces, gate_pre, up_pre):
+        row_scale, row_gate = block_facts(k, flip)
+        pre_a, pre_b = pre_a * row_scale, pre_b * row_scale
+        d_hidden = d_hidden_all[flip][k * span : (k + 1) * span] * row_gate
+        sig = jax.nn.sigmoid(pre_a)
+        d_a = (d_hidden * pre_b * sig * (1.0 + pre_a * (1.0 - sig))).astype(jnp.bfloat16)
+        d_b = (d_hidden * (pre_a * sig)).astype(jnp.bfloat16)
+        hidden_grads[flip, k] = (d_a, d_b)
 
-    def back(flip, m):
-        pieces = [
-            tuple(v[m * tok : (m + 1) * tok] for v in hidden_grads[flip, k]) for k in range(n_x)
-        ]
-        left = jnp.concatenate([a for a, b in pieces], axis=0)
-        right = jnp.concatenate([b for a, b in pieces], axis=0)
-        return contract_last(wg, left) + contract_last(wu, right)
+    order = [
+        tuple(v[m * tok : (m + 1) * tok] for v in hidden_grads[flip, k])
+        for flip in reversed(range(CORES))
+        for m in range(micro)
+        for k in range(n_x)
+    ]
+    left = jnp.concatenate([a for a, b in order], axis=0)
+    right = jnp.concatenate([b for a, b in order], axis=0)
+    back = contract_last(wg, left) + contract_last(wu, right)
+    half = n_x * span
+    block = n_x * tok
+    kept = back[:, half:]
+    others = [
+        sibling(back[:, m * block : (m + 1) * block].astype(jnp.bfloat16)) for m in range(micro)
+    ]
 
     def scatter(value):
         return lax.psum_scatter(value, "pipe", scatter_dimension=0, tiled=True)
 
-    others = [sibling(back(1, m).astype(jnp.bfloat16)) for m in reversed(range(micro))][::-1]
     norms = [None] * micro
     for m in reversed(range(micro)):
-        chip_sum = back(0, m) + others[m].astype(jnp.float32)
+        chip_sum = kept[:, m * block : (m + 1) * block] + others[m].astype(jnp.float32)
         if m == 0 and micro > 1:
             total = chip_sum[:, :tok]
             for k in range(1, n_x):

time: 515 us -> 459 us (0.89)
  matrix products: 191 us -> 121 us
  blocking collectives: 92.3 us -> 52.8 us
  waiting for transfers between devices: 186 us -> 224 us
  other arithmetic: 12.6 us -> 21.4 us
  local copies, waits for them, and re-layouts: 5.72 us -> 12.9 us
    dot_general x10 -> x4, matrix products: 135 us -> 74.4 us  [contract_last(): lax.dot_general(left, right, (((1,), (1,)), ((), ())), preferred_element_...]
    ppermute x4, waiting for transfers between devices: 44.7 us -> 94.1 us  [across(): return lax.ppermute(value, 'expert', pairs)]
    all_gather x1, blocking collectives: 47.2 us -> 5.19 us  [body(): facts = lax.all_gather(facts, 'expert', axis=0)]
    all_gather x1, waiting for transfers between devices: 49.9 us -> 21.7 us  [body(): mine = lax.all_gather(gained, 'pipe', axis=1, tiled=True)]
    reduce_scatter x2, waiting for transfers between devices: 70.9 us -> 95.1 us  [scatter(): return lax.psum_scatter(value, 'pipe', scatter_dimension=0, tiled=True)]
    all_gather x1, waiting for transfers between devices: 20 us -> 3.07 us  [body(): grads = lax.all_gather(grads, 'pipe', axis=1, tiled=True)]
    dot_general x8, matrix products: 56.5 us -> 46.1 us  [rows_dot(): lax.dot_general(left, right, (((1,), (0,)), ((), ())), preferred_element_...]
    ppermute x5, waiting for transfers between devices: 0.01 us -> 9.71 us  [sibling(): return lax.ppermute(value, 'expert', [(i, i ^ 1) for i in range(n_experts)])]
  transfers between devices with their start and end apart: 13 -> 13, of which waited for: 6 -> 9; matrix products, arithmetic and copies ran while one was open for 32% -> 15% of each run, Pallas kernels for 0% -> 0%
where the time goes in v2:
time: 459 us; the launch traced here: 454 us
  waiting for transfers between devices  224 us (49%)
  matrix products  121 us (26%)
  blocking collectives  52.8 us (12%)
  other arithmetic  21.4 us (5%)
  between operations  14.3 us (3%)
  local copies, waits for them, and re-layouts  12.9 us (3%)
  starting transfers between devices  8.39 us (2%)
    reduce_scatter x2, waiting for transfers between devices, scatter(): return lax.psum_scatter(value, 'pipe', scatter_dimension=0, tiled=True)  95.1 us
    ppermute x4, waiting for transfers between devices, across(): return lax.ppermute(value, 'expert', pairs)  94.1 us
    dot_general x4, matrix products, contract_last(): lax.dot_general(left, right, (((1,), (1,)), ((), ())), preferred_element_...  74.4 us
    dot_general x8, matrix products, rows_dot(): lax.dot_general(left, right, (((1,), (0,)), ((), ())), preferred_element_...  46.1 us
    psum x1, blocking collectives, body(): squares = lax.psum(jnp.sum(inputs * inputs, axis=-1), 'pipe')  22.1 us
    all_gather x1, waiting for transfers between devices, body(): mine = lax.all_gather(gained, 'pipe', axis=1, tiled=True)  21.7 us
    psum x1, blocking collectives, body(): inner = lax.psum(jnp.sum(scaled * inputs, axis=-1), 'pipe')  19.3 us
    ppermute x5, waiting for transfers between devices, sibling(): return lax.ppermute(value, 'expert', [(i, i ^ 1) for i in range(n_experts)])  9.71 us
  transfers between devices with their start and end apart: 13, of which 9 were waited for; matrix products, arithmetic and copies ran while one was open for 15% of the time, Pallas kernels for 0%

profile of v2, /device:TPU:0, one launch (start us, length us, event | category | flops | bytes accessed | tf_op | source)
XLA Modules:
  0.0 454.1 jit_solution(17238855736482330917)
XLA Ops:
  7.2 1.9 fusion.25
  9.2 3.0 collective-permute-start
  12.2 9.3 %collective-permute-done = bf16[256,768]{1,0:T(8,128)(2,1)S(1)} collective-permute-done((bf16[256,768]{1,0:T(8,128)(2,1)}, bf16[256,768]{1,0:T(8,128)(2,1)S(1)}, u32[]{:S(2)}, u32[]{:S(2)}) %collective-permute-start) | collective-permute-done | bytes 393248 | tf_op jit(solution)/shard_map/ppermute | solution.py:36
  21.5 1.9 pad_maximum_fusion
  23.5 22.1 %psum.21 = f32[2,128]{1,0:T(2,128)S(1)} all-reduce(f32[2,128]{1,0:T(2,128)S(1)} %get-tuple-element.42), channel_id=1, replica_groups=mesh['pipe'=8,'expert'=4] {'pipe'}, use_global_device_ids=true, to_apply=%region_1.0 | all-reduce | flops 256 | bytes 2048 | tf_op jit(solution)/shard_map/psum | solution.py:49
  46.7 5.2 %all_gather.11 = f32[4,5,256]{2,1,0:T(8,128)S(1)} all-gather(f32[1,5,256]{2,1,0:T(8,128)S(1)} %pad_maximum_fusion.2), channel_id=1, replica_groups=mesh['pipe'=8,'expert'=4] {'expert'}, dimensions={0}, use_global_device_ids=true | all-gather | bytes 25600 | tf_op jit(solution)/shard_map/all_gather | solution.py:55
  51.9 21.7 %all-gather.5.cloned.1.call-done = bf16[256,6144]{1,0:T(8,128)(2,1)} async-done(((bf16[256,768]{1,0:T(8,128)(2,1)}), bf16[256,6144]{1,0:T(8,128)(2,1)}) %all-gather.5.cloned.1.call-update) | async-done | bytes 3145744 | tf_op jit(solution)/shard_map/all_gather | solution.py:45
  73.6 1.5 collective-permute-start.1
  75.1 10.1 %fusion.11 = f32[256,1024]{1,0:T(8,128)} fusion(bf16[256,6144]{1,0:T(8,128)(2,1)} %all-gather.5.cloned.1.call-done, bf16[1,6144,1024]{2,1,0:T(8,128)(2,1)} %param.12), kind=kOutput, calls=%fused_computation.12 | convolution fusion | flops 3221225472 | bytes 16777216 | tf_op jit(solution)/shard_map/dot_general | solution.py:11
  85.2 7.8 %fusion.21 = f32[256,1024]{1,0:T(8,128)} fusion(bf16[256,6144]{1,0:T(8,128)(2,1)S(1)} %copy-done.13, bf16[1,6144,1024]{2,1,0:T(8,128)(2,1)} %param.11), kind=kOutput, calls=%fused_computation.22 | convolution fusion | flops 3221225472 | bytes 16777216 | tf_op jit(solution)/shard_map/dot_general | solution.py:11
  93.0 49.6 %collective-permute-done.1 = bf16[256,6144]{1,0:T(8,128)(2,1)S(1)} collective-permute-done((bf16[256,6144]{1,0:T(8,128)(2,1)}, bf16[256,6144]{1,0:T(8,128)(2,1)S(1)}, u32[]{:S(2)}, u32[]{:S(2)}) %collective-permute-start.1) | collective-permute-done | bytes 3145760 | tf_op jit(solution)/shard_map/ppermute | solution.py:36
  142.6 5.5 %fusion.7 = f32[256,1024]{1,0:T(8,128)S(1)} fusion(bf16[256,6144]{1,0:T(8,128)(2,1)} %collective-permute-done.2, bf16[1,6144,1024]{2,1,0:T(8,128)(2,1)S(1)} %bitcast.85), kind=kOutput, calls=%fused_computation.8 | convolution fusion | flops 3221225472 | bytes 16777216 | tf_op jit(solution)/shard_map/dot_general | solution.py:11
  148.1 5.5 %fusion.17 = f32[256,1024]{1,0:T(8,128)S(1)} fusion(bf16[256,6144]{1,0:T(8,128)(2,1)} %collective-permute-done.2, bf16[1,6144,1024]{2,1,0:T(8,128)(2,1)S(1)} %bitcast.83), kind=kOutput, calls=%fused_computation.18 | convolution fusion | flops 3221225472 | bytes 16777216 | tf_op jit(solution)/shard_map/dot_general | solution.py:11
  153.6 4.5 fusion.9
  158.1 4.5 fusion.19
  162.5 3.9 fusion.5
  166.4 4.5 fusion.15
  170.9 3.1 all-gather.3.cloned.1.call-done
  174.1 11.7 %fusion = f32[512,1024]{1,0:T(8,128)S(1)} fusion(bf16[512,6144]{1,0:T(8,128)(2,1)} %all-gather.3.cloned.1.call-done, bf16[1,1024,6144]{2,1,0:T(8,128)(2,1)} %param.13), kind=kOutput, calls=%fused_computation.1 | convolution fusion | flops 6442450944 | bytes 20971520 | tf_op jit(solution)/shard_map/dot_general | solution.py:17
  185.8 1.2 multiply_convert_fusion
  187.0 11.8 %fusion.2 = f32[512,1024]{1,0:T(8,128)S(1)} fusion(bf16[512,6144]{1,0:T(8,128)(2,1)} %collective-permute-done.4, bf16[1,1024,6144]{2,1,0:T(8,128)(2,1)} %param.13), kind=kOutput, calls=%fused_computation.3 | convolution fusion | flops 6442450944 | bytes 20971520 | tf_op jit(solution)/shard_map/dot_general | solution.py:17
  198.8 1.2 multiply_convert_fusion.2
  200.0 0.7 slice_dynamic-update-slice_fusion.15
  200.7 0.7 slice_dynamic-update-slice_fusion.14
  202.2 0.7 slice_dynamic-update-slice_fusion.4
  203.1 0.7 slice_dynamic-update-slice_fusion.11
  203.8 0.7 slice_dynamic-update-slice_fusion.10
  204.6 0.7 slice_dynamic-update-slice_fusion.9
  205.3 0.7 slice_dynamic-update-slice_fusion.8
  206.0 21.3 %fusion.13 = f32[1024,6144]{1,0:T(8,128)} fusion(bf16[1024,1024]{1,0:T(8,128)(2,1)} %slice_dynamic-update-slice_fusion.8, bf16[1,6144,1024]{2,1,0:T(8,128)(2,1)} %param.11), kind=kOutput, calls=%fused_computation.14 | convolution fusion | flops 12884901888 | bytes 39845888 | tf_op jit(solution)/shard_map/dot_general | solution.py:17
  227.3 29.7 %fusion.38 = (bf16[6144,1024]{0,1:T(8,128)(2,1)}, f32[6144,1024]{0,1:T(8,128)}) fusion(f32[1024,6144]{1,0:T(8,128)} %fusion.13, bf16[1024,1024]{1,0:T(8,128)(2,1)S(1)} %slice_dynamic-update-slice_fusion, bf16[1,6144,1024]{2,1,0:T(8,128)(2,1)} %param.12), kind=kOutput, calls=%fused_computation.117 | convolution fusion | flops 12897484800 | bytes 77594624 | tf_op jit(solution)/shard_map/dot_general | solution.py:17
  257.0 3.3 fusion.37
  260.9 5.2 %collective-permute-done.5 = bf16[6144,256]{0,1:T(8,128)(2,1)S(1)} collective-permute-done((bf16[6144,256]{0,1:T(8,128)(2,1)S(1)}, bf16[6144,256]{0,1:T(8,128)(2,1)S(1)}, u32[]{:S(2)}, u32[]{:S(2)}) %collective-permute-start.5) | collective-permute-done | bytes 3145760 | tf_op jit(solution)/shard_map/ppermute | solution.py:39
  266.1 4.5 collective-permute-done.7
  270.6 7.7 %slice_add_fusion.1 = (f32[6144,256]{0,1:T(8,128)}, bf16[6144,256]{0,1:T(8,128)(2,1)}) fusion(f32[6144,1024]{0,1:T(8,128)} %get-tuple-element.55, bf16[6144,256]{0,1:T(8,128)(2,1)S(1)} %collective-permute-done.5, bf16[6144,256]{0,1:T(8,128)(2,1)S(1)} %collective-permute-done.7), kind=kLoop, calls=%fused_computation.26 | loop fusion | flops 7864320 | bytes 28311552 | tf_op jit(solution)/shard_map/add | solution.py:108
  278.4 2.1 slice.291
  280.5 1.5 collective-permute-start.6
  282.0 35.2 %collective-permute-done.6 = bf16[6144,128]{0,1:T(8,128)(2,1)S(1)} collective-permute-done((bf16[6144,128]{0,1:T(8,128)(2,1)S(1)}, bf16[6144,128]{0,1:T(8,128)(2,1)S(1)}, u32[]{:S(2)}, u32[]{:S(2)}) %collective-permute-start.6) | collective-permute-done | bytes 1572896 | tf_op jit(solution)/shard_map/ppermute | solution.py:36
  317.2 3.5 fusion.24
  320.8 30.4 %reduce-scatter.5.cloned.1.call-done = bf16[768,256]{0,1:T(8,128)(2,1)} async-done(((bf16[6144,256]{0,1:T(8,128)(2,1)}), bf16[768,256]{0,1:T(8,128)(2,1)}) %reduce-scatter.5.cloned.1.call-update) | async-done | bytes 393232 | tf_op jit(solution)/shard_map/reduce_scatter | solution.py:104
  351.1 0.9 slice.245
  352.1 1.6 collective-permute-start.8
  353.6 64.8 %reduce-scatter.3.cloned.1.call-done = bf16[768,128]{0,1:T(8,128)(2,1)} async-done(((bf16[6144,128]{0,1:T(8,128)(2,1)}), bf16[768,128]{0,1:T(8,128)(2,1)}) %reduce-scatter.3.cloned.1.call-update) | async-done | bytes 196624 | tf_op jit(solution)/shard_map/reduce_scatter | solution.py:104
  418.4 1.0 convert_bitcast_fusion
  419.3 1.0 add_bitcast_fusion.1
  420.7 6.3 %psum.23 = f32[768]{0:T(1024)} all-reduce(f32[768]{0:T(1024)S(1)} %get-tuple-element.24), channel_id=1, replica_groups=mesh['pipe'=8,'expert'=4] {'expert'}, use_global_device_ids=true, to_apply=%region_7.8 | all-reduce | flops 768 | bytes 6144 | tf_op jit(solution)/shard_map/psum | solution.py:130
  426.9 19.3 %psum.22 = f32[2,128]{1,0:T(2,128)S(1)} all-reduce(f32[2,128]{1,0:T(2,128)S(1)} %get-tuple-element.25), channel_id=1, replica_groups=mesh['pipe'=8,'expert'=4] {'pipe'}, use_global_device_ids=true, to_apply=%region_5.6 | all-reduce | flops 256 | bytes 2048 | tf_op jit(solution)/shard_map/psum | solution.py:126
  446.3 1.1 fusion.29
  (73 shorter events, 3.3 us)
Async XLA Ops:
  7.2 39.0 %copy-start.11 = (s32[2,128,2]{1,2,0:T(2,128)S(1)}, s32[2,128,2]{1,2,0:T(2,128)}, u32[]{:S(2)}) copy-start(s32[2,128,2]{1,2,0:T(2,128)} %param.14) | copy-start | bytes 6148
  7.2 39.5 %copy-start.12 = (f32[2,128,2]{1,2,0:T(2,128)S(1)}, f32[2,128,2]{1,2,0:T(2,128)}, u32[]{:S(2)}) copy-start(f32[2,128,2]{1,2,0:T(2,128)} %param.15) | copy-start | bytes 6148
  7.2 66.5 %all-gather.5.cloned.1.call-start = ((), (), s32[]{:S(2)}) async-start(), calls=%async_computation.3 | async-start | bytes 3538944 | tf_op jit(solution)/shard_map/all_gather | solution.py:45
  9.1 164.9 %all-gather.3.cloned.1.call-start = ((), (), s32[]{:S(2)}) async-start(), calls=%async_computation.2 | async-start | bytes 7077888 | tf_op jit(solution)/shard_map/all_gather | solution.py:48
  9.2 12.3 %collective-permute-start = (bf16[256,768]{1,0:T(8,128)(2,1)}, bf16[256,768]{1,0:T(8,128)(2,1)S(1)}, u32[]{:S(2)}, u32[]{:S(2)}) collective-permute-start(bf16[256,768]{1,0:T(8,128)(2,1)} %bitcast.69), channel_id=1, source_target_pairs={{2,0},{3,1},{0,2},{1,3},{6,4},{7,5},{4,6},{5,7},{10,8},{11,9},{8,1... | collective-permute-start | bytes 1179656 | tf_op jit(solution)/shard_map/ppermute | solution.py:36
  23.5 327.7 %reduce-scatter.5.cloned.1.call-start = ((), (), s32[]{:S(2)}) async-start(), calls=%async_computation.5 | async-start | bytes 3538944 | tf_op jit(solution)/shard_map/reduce_scatter | solution.py:104
  46.1 0.6 copy-start.8
  73.6 11.6 %copy-start.13 = (bf16[256,6144]{1,0:T(8,128)(2,1)S(1)}, bf16[256,6144]{1,0:T(8,128)(2,1)}, u32[]{:S(2)}) copy-start(bf16[256,6144]{1,0:T(8,128)(2,1)} %all-gather.5.cloned.1.call-done) | copy-start | bytes 9437188
  73.6 68.9 %collective-permute-start.1 = (bf16[256,6144]{1,0:T(8,128)(2,1)}, bf16[256,6144]{1,0:T(8,128)(2,1)S(1)}, u32[]{:S(2)}, u32[]{:S(2)}) collective-permute-start(bf16[256,6144]{1,0:T(8,128)(2,1)} %all-gather.5.cloned.1.call-done), channel_id=1, source_target_pairs={{2,0},{3,1},{0,2},{1,3},{6,4},{7,5},{4,6},{5,7},{10,8},{11,9},{8,1... | collective-permute-start | bytes 9437192 | tf_op jit(solution)/shard_map/ppermute | solution.py:36
  75.1 67.5 %collective-permute-start.2 = (bf16[256,6144]{1,0:T(8,128)(2,1)}, bf16[256,6144]{1,0:T(8,128)(2,1)}, u32[]{:S(2)}, u32[]{:S(2)}) collective-permute-start(bf16[256,6144]{1,0:T(8,128)(2,1)} %all-gather.5.cloned.1.call-done), channel_id=1, source_target_pairs={{0,1},{1,0},{2,3},{3,2},{4,5},{5,4},{6,7},{7,6},{8,9},{9,8},{10,11... | collective-permute-start | bytes 9437192 | tf_op jit(solution)/shard_map/ppermute | solution.py:39
  75.1 67.5 %slice-start.3 = ((s8[12582912]{0:T(1024)(128)(4,1)}), s8[4194304]{0:T(1024)(128)(4,1)S(1)}, s32[]{:S(2)}) async-start(s8[12582912]{0:T(1024)(128)(4,1)} %bitcast.84), calls=%async_computation.9 | async-start | bytes 8388608
  75.1 67.5 %slice-start.4 = ((s8[12582912]{0:T(1024)(128)(4,1)}), s8[4194304]{0:T(1024)(128)(4,1)S(1)}, s32[]{:S(2)}) async-start(s8[12582912]{0:T(1024)(128)(4,1)} %bitcast.84), calls=%async_computation.10 | async-start | bytes 8388608
  85.2 57.4 %slice-start.5 = ((s8[12582912]{0:T(1024)(128)(4,1)}), s8[4194304]{0:T(1024)(128)(4,1)S(1)}, s32[]{:S(2)}) async-start(s8[12582912]{0:T(1024)(128)(4,1)} %bitcast.84), calls=%async_computation.11 | async-start | bytes 8388608
  85.2 62.9 %slice-start = ((s8[12582912]{0:T(1024)(128)(4,1)}), s8[4194304]{0:T(1024)(128)(4,1)S(1)}, s32[]{:S(2)}) async-start(s8[12582912]{0:T(1024)(128)(4,1)} %bitcast.82), calls=%async_computation.6 | async-start | bytes 8388608
  85.2 62.9 %slice-start.1 = ((s8[12582912]{0:T(1024)(128)(4,1)}), s8[4194304]{0:T(1024)(128)(4,1)S(1)}, s32[]{:S(2)}) async-start(s8[12582912]{0:T(1024)(128)(4,1)} %bitcast.82), calls=%async_computation.7 | async-start | bytes 8388608
  93.0 55.1 %slice-start.2 = ((s8[12582912]{0:T(1024)(128)(4,1)}), s8[4194304]{0:T(1024)(128)(4,1)S(1)}, s32[]{:S(2)}) async-start(s8[12582912]{0:T(1024)(128)(4,1)} %bitcast.82), calls=%async_computation.8 | async-start | bytes 8388608
  142.6 20.0 %collective-permute-start.3 = (bf16[256,6144]{1,0:T(8,128)(2,1)S(1)}, bf16[256,6144]{1,0:T(8,128)(2,1)S(1)}, u32[]{:S(2)}, u32[]{:S(2)}) collective-permute-start(bf16[256,6144]{1,0:T(8,128)(2,1)S(1)} %collective-permute-done.1), channel_id=1, source_target_pairs={{0,1},{1,0},{2,3},{3,2},{4,5},{5,4},{6,7},{7,6},{8,9},{9,8},{10,11... | collective-permute-start | bytes 9437192 | tf_op jit(solution)/shard_map/ppermute | solution.py:39
  174.0 13.0 %collective-permute-start.4 = (bf16[512,6144]{1,0:T(8,128)(2,1)}, bf16[512,6144]{1,0:T(8,128)(2,1)}, u32[]{:S(2)}, u32[]{:S(2)}) collective-permute-start(bf16[512,6144]{1,0:T(8,128)(2,1)} %all-gather.3.cloned.1.call-done), channel_id=1, source_target_pairs={{0,1},{1,0},{2,3},{3,2},{4,5},{5,4},{6,7},{7,6},{8,9},{9,8},{10,11... | collective-permute-start | bytes 18874376 | tf_op jit(solution)/shard_map/ppermute | solution.py:39
  174.0 11.7 %copy-start.3 = (f32[256,1024]{1,0:T(8,128)S(1)}, f32[256,1024]{1,0:T(8,128)}, u32[]{:S(2)}) copy-start(f32[256,1024]{1,0:T(8,128)} %fusion.11) | copy-start | bytes 3145732
  174.0 11.7 %copy-start.4 = (f32[256,1024]{1,0:T(8,128)S(1)}, f32[256,1024]{1,0:T(8,128)}, u32[]{:S(2)}) copy-start(f32[256,1024]{1,0:T(8,128)} %fusion.21) | copy-start | bytes 3145732
  174.0 11.7 %copy-start.5 = (f32[256,1024]{1,0:T(8,128)S(1)}, f32[256,1024]{1,0:T(8,128)}, u32[]{:S(2)}) copy-start(f32[256,1024]{1,0:T(8,128)} %fusion.9) | copy-start | bytes 3145732
  174.1 11.7 %copy-start.6 = (f32[256,1024]{1,0:T(8,128)S(1)}, f32[256,1024]{1,0:T(8,128)}, u32[]{:S(2)}) copy-start(f32[256,1024]{1,0:T(8,128)} %fusion.19) | copy-start | bytes 3145732
  187.0 11.8 %copy-start.2 = (f32[256,1024]{1,0:T(8,128)S(1)}, f32[256,1024]{1,0:T(8,128)}, u32[]{:S(2)}) copy-start(f32[256,1024]{1,0:T(8,128)} %fusion.15) | copy-start | bytes 3145732
  260.3 5.9 %collective-permute-start.5 = (bf16[6144,256]{0,1:T(8,128)(2,1)S(1)}, bf16[6144,256]{0,1:T(8,128)(2,1)S(1)}, u32[]{:S(2)}, u32[]{:S(2)}) collective-permute-start(bf16[6144,256]{0,1:T(8,128)(2,1)S(1)} %get-tuple-element.28), channel_id=1, source_target_pairs={{0,1},{1,0},{2,3},{3,2},{4,5},{5,4},{6,7},{7,6},{8,9},{9,8},{10,11... | collective-permute-start | bytes 9437192 | tf_op jit(solution)/shard_map/ppermute | solution.py:39
  260.8 9.8 %collective-permute-start.7 = (bf16[6144,256]{0,1:T(8,128)(2,1)S(1)}, bf16[6144,256]{0,1:T(8,128)(2,1)S(1)}, u32[]{:S(2)}, u32[]{:S(2)}) collective-permute-start(bf16[6144,256]{0,1:T(8,128)(2,1)S(1)} %get-tuple-element.29), channel_id=1, source_target_pairs={{0,1},{1,0},{2,3},{3,2},{4,5},{5,4},{6,7},{7,6},{8,9},{9,8},{10,11... | collective-permute-start | bytes 9437192 | tf_op jit(solution)/shard_map/ppermute | solution.py:39
  278.4 140.0 %reduce-scatter.3.cloned.1.call-start = ((), (), s32[]{:S(2)}) async-start(), calls=%async_computation.4 | async-start | bytes 1769472 | tf_op jit(solution)/shard_map/reduce_scatter | solution.py:104
  280.5 36.7 %collective-permute-start.6 = (bf16[6144,128]{0,1:T(8,128)(2,1)S(1)}, bf16[6144,128]{0,1:T(8,128)(2,1)S(1)}, u32[]{:S(2)}, u32[]{:S(2)}) collective-permute-start(bf16[6144,128]{0,1:T(8,128)(2,1)S(1)} %slice.291), channel_id=1, source_target_pairs={{2,0},{3,1},{0,2},{1,3},{6,4},{7,5},{4,6},{5,7},{10,8},{11,9},{8,1... | collective-permute-start | bytes 4718600 | tf_op jit(solution)/shard_map/ppermute | solution.py:36
  320.7 99.6 %copy-start = (bf16[2,128,768]{2,1,0:T(8,128)(2,1)S(1)}, bf16[2,128,768]{2,1,0:T(8,128)(2,1)}, u32[]{:S(2)}) copy-start(bf16[2,128,768]{2,1,0:T(8,128)(2,1)} %param.8) | copy-start | bytes 1179652
  320.7 99.6 %copy-start.7 = (f32[768]{0:T(1024)S(1)}, f32[768]{0:T(1024)}, u32[]{:S(2)}) copy-start(f32[768]{0:T(1024)} %param.10) | copy-start | bytes 9220
  320.7 99.6 %copy-start.9 = (f32[2,128]{1,0:T(2,128)S(1)}, f32[2,128]{1,0:T(2,128)}, u32[]{:S(2)}) copy-start(f32[2,128]{1,0:T(2,128)} %copy-done.8) | copy-start | bytes 3076
  320.7 125.5 %copy-start.1 = (bf16[2,128,768]{2,1,0:T(8,128)(2,1)S(1)}, bf16[2,128,768]{2,1,0:T(8,128)(2,1)}, u32[]{:S(2)}) copy-start(bf16[2,128,768]{2,1,0:T(8,128)(2,1)} %param.9) | copy-start | bytes 1179652
  320.7 125.5 %copy-start.10 = (f32[2,128]{1,0:T(2,128)S(1)}, f32[2,128]{1,0:T(2,128)}, u32[]{:S(2)}) copy-start(f32[2,128]{1,0:T(2,128)} %get-tuple-element.52) | copy-start | bytes 3076
  352.1 67.3 %collective-permute-start.8 = (bf16[768,128]{0,1:T(8,128)(2,1)S(1)}, bf16[768,128]{0,1:T(8,128)(2,1)S(1)}, u32[]{:S(2)}, u32[]{:S(2)}) collective-permute-start(bf16[768,128]{0,1:T(8,128)(2,1)S(1)} %slice.245), channel_id=1, source_target_pairs={{2,0},{3,1},{0,2},{1,3},{6,4},{7,5},{4,6},{5,7},{10,8},{11,9},{8,1... | collective-permute-start | bytes 589832 | tf_op jit(solution)/shard_map/ppermute | solution.py:36
Sparse Core Ops, SparseCore 0:
  10.2 63.3 all-gather.4
  76.4 97.5 all-gather.2
  278.5 72.5 reduce-scatter.4
  354.4 63.9 reduce-scatter.2
